TPU v7x, 32 devices: a whole 2x2x4 slice. The times are simulated.
32 devices in a mesh: vp: 8 (over y, x, core), ob: 4 (over z).
Axes of the slice: x: 2, y: 2, z: 4, core: 2. Of those that a mesh axis runs over, the one named last changes fastest.
Arguments:
- integrals: bfloat16 [147456, 2304], P('vp'), may hold values from -0.125 to 0.125
- amplitudes: bfloat16 [2304, 2048], P('vp', 'ob'), may hold values from -12 to 12
- rotation: bfloat16 [384, 384], replicated, may hold values from -0.3125 to 0.3125
- eps_occ: float32 [64], replicated, may hold values from -2.5 to -0.5
- eps_vir: float32 [384], replicated, may hold values from 0.2 to 4
Outputs:
- update: bfloat16 [2048, 147456], P('ob', 'vp')
All inputs are finite; a program needn't handle non-finite values.
Results may differ from a plain program's by a relative error of at most 0.0058.
Values may be sent and summed in bfloat16 or wider, within the bound.
A program may use at most 192 MiB of HBM per device.

v0:
```python
import functools

import jax
import jax.numpy as jnp
from jax import lax
from jax.experimental import pallas as pl
from jax.experimental.pallas import tpu as pltpu
from jax.sharding import PartitionSpec as P

LANES = 128
ROWS = 16
SLOTS = 3


def pair_energy(eps_occ, first_pair, pair_count):
    occupied = eps_occ.shape[0]
    pair_index = first_pair + jnp.arange(pair_count, dtype=jnp.int32)
    first_orbital = pair_index // occupied
    second_orbital = pair_index % occupied
    orbitals = jnp.arange(occupied, dtype=jnp.int32)
    first_energy = jnp.sum(
        jnp.where(orbitals[None, :] == first_orbital[:, None], eps_occ[None, :], 0.0), axis=1
    )
    second_energy = jnp.sum(
        jnp.where(orbitals[None, :] == second_orbital[:, None], eps_occ[None, :], 0.0), axis=1
    )
    return first_energy + second_energy


def ladder_kernel(
    peers,
    gather,
    amplitudes,
    integrals,
    rotation,
    rotation_t,
    energy,
    eps_column,
    eps_row,
    out,
    landed,
    panels,
    tiles,
    spread,
    sending,
    halves,
    dressed,
    updates,
    packed,
    panel_send,
    panel_recv,
    own_sem,
    tile_sem,
    half_send,
    half_recv,
    load_sem,
    update_send,
    update_recv,
):
    chunks, _, width = amplitudes.shape
    row_count, summed = integrals.shape
    orbitals = rotation.shape[0]
    _, groups, per_owner, group_rows, _ = landed.shape
    chunk_pairs = per_owner // chunks
    first_rows = row_count // orbitals
    strips = orbitals // LANES
    batches = per_owner // ROWS
    per_chunk = batches // chunks
    steps = chunks * first_rows
    me = lax.axis_index("vp")

    def peer_of(step):
        return lax.rem(me + step, peers)

    def each_peer(body):
        def run(step, carry):
            body(step, peer_of(step))
            return carry

        lax.fori_loop(1, peers, run, 0)

    barrier = pltpu.get_barrier_semaphore()
    each_peer(lambda step, peer: pl.semaphore_signal(barrier, inc=1, device_id={"vp": peer}))

    def fetch(step):
        first = pl.multiple_of(lax.rem(step, first_rows) * orbitals, orbitals)
        slot = lax.rem(step, SLOTS)
        return pltpu.make_async_copy(
            integrals.at[pl.ds(first, orbitals)], tiles.at[slot], tile_sem.at[slot]
        )

    for step in range(min(SLOTS - 1, steps)):
        fetch(step).start()
    pl.semaphore_wait(barrier, peers - 1)

    def panel_copy(chunk, step, peer, origin):
        return pltpu.make_async_remote_copy(
            src_ref=amplitudes.at[chunk],
            dst_ref=panels.at[chunk, origin],
            send_sem=panel_send.at[chunk, step],
            recv_sem=panel_recv.at[chunk, origin],
            device_id={"vp": peer},
        )

    def own_panel(chunk):
        return pltpu.make_async_copy(
            amplitudes.at[chunk], panels.at[chunk, me if gather else 0], own_sem
        )

    for chunk in range(chunks):
        if gather:
            each_peer(lambda step, peer: panel_copy(chunk, step, peer, me).start())
        own_panel(chunk).start()
        own_panel(chunk).wait()
        if gather and chunk == 0:
            each_peer(lambda step, peer: panel_copy(0, step, peer, peer).wait_recv())

    def half_copy(turn, step, peer, origin):
        chunk, group = lax.div(turn, groups), lax.rem(turn, groups)
        slot = lax.rem(turn, 2)
        return pltpu.make_async_remote_copy(
            src_ref=sending.at[slot, pl.ds(peer * chunk_pairs, chunk_pairs)],
            dst_ref=landed.at[origin, group, pl.ds(chunk * chunk_pairs, chunk_pairs)],
            send_sem=half_send.at[slot, step],
            recv_sem=half_recv.at[turn, origin],
            device_id={"vp": peer},
        )

    def send_turn(turn, carry):
        chunk, group = lax.div(turn, groups), lax.rem(turn, groups)
        slot = lax.rem(turn, 2)
        if gather:
            for later in range(1, chunks):

                @pl.when(turn == later * groups)
                def _():
                    each_peer(lambda step, peer: panel_copy(later, step, peer, peer).wait_recv())

        def one_row(row, carry):
            step = turn * group_rows + row
            fetch(step).wait()

            @pl.when(step + (SLOTS - 1) < steps)
            def _():
                fetch(step + (SLOTS - 1)).start()

            ladder = jnp.dot(
                tiles[lax.rem(step, SLOTS)],
                panels[chunk].reshape(summed, width),
                preferred_element_type=jnp.float32,
            )
            half = jnp.dot(
                ladder.T.astype(jnp.bfloat16), rotation[...], preferred_element_type=jnp.float32
            )
            for strip in range(strips):
                spread[strip, pl.ds(row, width, stride=group_rows), :] = half[
                    :, strip * LANES : (strip + 1) * LANES
                ]
            return carry

        lax.fori_loop(0, group_rows, one_row, 0)

        @pl.when(turn >= 2)
        def _():
            each_peer(lambda step, peer: half_copy(turn - 2, step, peer, me).wait_send())

        def narrow(pair, carry):
            first = pl.multiple_of(pair * group_rows, group_rows)
            for strip in range(strips):
                sending[slot, pair, :, pl.ds(strip * LANES, LANES)] = spread[
                    strip, pl.ds(first, group_rows), :
                ].astype(jnp.bfloat16)
            return carry

        lax.fori_loop(0, width, narrow, 0, unroll=8)
        each_peer(lambda step, peer: half_copy(turn, step, peer, me).start())
        own = pltpu.make_async_copy(
            sending.at[slot, pl.ds(me * chunk_pairs, chunk_pairs)],
            landed.at[me, group, pl.ds(chunk * chunk_pairs, chunk_pairs)],
            own_sem,
        )
        own.start()
        own.wait()
        return carry

    turns = chunks * groups
    lax.fori_loop(0, turns, send_turn, 0)

    def update_copy(batch, step, peer, origin):
        slot = lax.rem(batch, 2)
        return pltpu.make_async_remote_copy(
            src_ref=updates.at[slot, :, pl.ds(pl.multiple_of(peer * row_count, LANES), row_count)],
            dst_ref=out.at[pl.ds(pl.multiple_of(origin * per_owner + batch * ROWS, ROWS), ROWS)],
            send_sem=update_send.at[slot, step],
            recv_sem=update_recv.at[batch, origin],
            device_id={"vp": peer},
        )

    def return_batch(batch, carry):
        slot = lax.rem(batch, 2)
        chunk = lax.div(batch, per_chunk)

        @pl.when(lax.rem(batch, per_chunk) == 0)
        def _():
            def arrived(group, carry):
                each_peer(
                    lambda step, peer: half_copy(
                        chunk * groups + group, step, peer, peer
                    ).wait_recv()
                )
                return carry

            lax.fori_loop(0, groups, arrived, 0)

        load = pltpu.make_async_copy(
            landed.at[:, :, pl.ds(batch * ROWS, ROWS)], halves, load_sem
        )
        load.start()
        load.wait()

        def one_pair(pair, carry):
            if group_rows % ROWS == 0:
                half = halves[:, :, pair].reshape(orbitals, orbitals)
            else:
                for origin in range(peers):
                    for group in range(groups):
                        packed[pl.ds((origin * groups + group) * group_rows, group_rows), :] = (
                            halves[origin, group, pair].astype(jnp.float32)
                        )
                half = packed[...].astype(jnp.bfloat16)
            full = jnp.dot(rotation_t[...], half, preferred_element_type=jnp.float32)
            divisor = energy[batch * ROWS + pair] - eps_column[...] - eps_row[...]
            full = full / divisor
            first = pl.multiple_of(pair * orbitals, orbitals)
            for strip in range(strips):
                dressed[strip, pl.ds(first, orbitals), :] = full[
                    :, strip * LANES : (strip + 1) * LANES
                ]
            return carry

        lax.fori_loop(0, ROWS, one_pair, 0)

        @pl.when(batch >= 2)
        def _():
            each_peer(lambda step, peer: update_copy(batch - 2, step, peer, me).wait_send())

        def lay_out(orbital, carry):
            for strip in range(strips):
                column = pl.multiple_of(orbital * orbitals + strip * LANES, LANES)
                updates[slot, :, pl.ds(column, LANES)] = dressed[
                    strip, pl.ds(orbital, ROWS, stride=orbitals), :
                ].astype(jnp.bfloat16)
            return carry

        lax.fori_loop(0, orbitals, lay_out, 0, unroll=8)
        each_peer(lambda step, peer: update_copy(batch, step, peer, me).start())
        own = pltpu.make_async_copy(
            updates.at[slot, :, pl.ds(pl.multiple_of(me * row_count, LANES), row_count)],
            out.at[pl.ds(pl.multiple_of(me * per_owner + batch * ROWS, ROWS), ROWS)],
            own_sem,
        )
        own.start()
        own.wait()
        return carry

    lax.fori_loop(0, batches, return_batch, 0)

    if gather:
        for chunk in range(chunks):
            each_peer(lambda step, peer: panel_copy(chunk, step, peer, me).wait_send())
    for turn in range(max(0, turns - 2), turns):
        each_peer(lambda step, peer: half_copy(turn, step, peer, me).wait_send())
    for batch in range(max(0, batches - 2), batches):
        each_peer(lambda step, peer: update_copy(batch, step, peer, me).wait_send())

    def all_arrived(batch, carry):
        each_peer(lambda step, peer: update_copy(batch, step, peer, peer).wait_recv())
        return carry

    lax.fori_loop(0, batches, all_arrived, 0)


def shards(integrals, amplitudes, rotation, eps_occ, eps_vir):
    row_count, summed = integrals.shape
    depth, pair_count = amplitudes.shape
    orbitals = rotation.shape[0]
    peers = lax.axis_size("vp")
    per_owner = pair_count // peers
    first_rows = row_count // orbitals
    group_rows = ROWS if first_rows % ROWS == 0 else first_rows
    groups = first_rows // group_rows
    chunks = 2 if per_owner % (2 * ROWS) == 0 else 1
    chunk_pairs = per_owner // chunks
    width = peers * chunk_pairs
    batches = per_owner // ROWS
    turns = chunks * groups
    gather = depth % ROWS == 0
    if not gather:
        amplitudes = lax.all_gather(amplitudes, "vp", axis=0, tiled=True)
        depth = summed
    amplitudes = (
        amplitudes.reshape(depth, peers, chunks, chunk_pairs)
        .transpose(2, 0, 1, 3)
        .reshape(chunks, depth, width)
    )
    first_pair = lax.axis_index("ob") * pair_count + lax.axis_index("vp") * per_owner
    energy = pair_energy(eps_occ, first_pair, per_owner)
    bf16, f32 = jnp.bfloat16, jnp.float32
    vmem = pl.BlockSpec(memory_space=pltpu.VMEM)
    anywhere = pl.BlockSpec(memory_space=pl.ANY)
    spare = (LANES, LANES) if group_rows % ROWS == 0 else (orbitals, orbitals)
    flops = 2 * row_count * summed * pair_count + 4 * pair_count * row_count * orbitals
    result, _ = pl.pallas_call(
        functools.partial(ladder_kernel, peers, gather),
        out_shape=(
            jax.ShapeDtypeStruct((pair_count, row_count), bf16),
            jax.ShapeDtypeStruct((peers, groups, per_owner, group_rows, orbitals), bf16),
        ),
        in_specs=[
            anywhere,
            anywhere,
            vmem,
            vmem,
            pl.BlockSpec(memory_space=pltpu.SMEM),
            vmem,
            vmem,
        ],
        out_specs=(anywhere, anywhere),
        scratch_shapes=[
            pltpu.VMEM((chunks, summed // depth, depth, width), bf16),
            pltpu.VMEM((SLOTS, orbitals, summed), bf16),
            pltpu.VMEM((orbitals // LANES, width * group_rows, LANES), f32),
            pltpu.VMEM((2, width, group_rows, orbitals), bf16),
            pltpu.VMEM((peers, groups, ROWS, group_rows, orbitals), bf16),
            pltpu.VMEM((orbitals // LANES, ROWS * orbitals, LANES), f32),
            pltpu.VMEM((2, ROWS, orbitals * orbitals), bf16),
            pltpu.VMEM(spare, f32),
            pltpu.SemaphoreType.DMA((chunks, peers)),
            pltpu.SemaphoreType.DMA((chunks, peers)),
            pltpu.SemaphoreType.DMA,
            pltpu.SemaphoreType.DMA((SLOTS,)),
            pltpu.SemaphoreType.DMA((2, peers)),
            pltpu.SemaphoreType.DMA((turns, peers)),
            pltpu.SemaphoreType.DMA,
            pltpu.SemaphoreType.DMA((2, peers)),
            pltpu.SemaphoreType.DMA((batches, peers)),
        ],
        cost_estimate=pl.CostEstimate(
            flops=flops, bytes_accessed=chunks * 2 * row_count * summed, transcendentals=0
        ),
        compiler_params=pltpu.CompilerParams(
            collective_id=0, has_side_effects=True, vmem_limit_bytes=60 * 1024 * 1024
        ),
    )(
        amplitudes,
        integrals,
        rotation,
        rotation.T,
        energy,
        eps_vir.reshape(orbitals, 1),
        eps_vir.reshape(1, orbitals),
    )
    return result


def solution(mesh):
    return jax.shard_map(
        shards,
        mesh=mesh,
        in_specs=(P("vp", None), P("vp", "ob"), P(), P(), P()),
        out_specs=P("ob", "vp"),
        check_vma=False,
    )
```

profile of v0, /device:TPU:1, one launch (start us, length us, event | category | flops | bytes accessed | tf_op | source)
XLA Modules:
  0.0 471.2 jit_solution(10620267100475307718)
XLA Ops:
  0.0 0.8 select_reduce_fusion
  0.9 0.6 add.38.energy
  1.4 1.3 reshape.48.eps_row
  2.7 1.5 reshape.49.eps_column
  4.1 1.9 copy.15
  6.0 1.2 copy.13
  7.2 0.9 copy.16.amplitudes
  8.1 446.1 %shard_map.55 = (bf16[512,18432]{1,0:T(8,128)(2,1)}, bf16[8,3,64,16,384]{4,3,2,1,0:T(8,128)(2,1)}) custom-call(bf16[2,288,256]{2,1,0:T(8,128)(2,1)} %copy.16.amplitudes, bf16[18432,2304]{1,0:T(8,128)(2,1)} %integrals.1, bf16[384,384]{1,0:T(8,128)(2,1)} %rotation.1, bf16[384,384]{1,0:T(8,128)(2,1)} %bitcast.7, f32[64]{0:T(128)} %add.38.energy, ...), custom_call_target="tpu_custom_call" | custom-call | flops 57982058496 | bytes 169869312 | tf_op jit(solution)/shard_map/pallas_call | solution.py:313
  454.3 16.9 %copy.19 = bf16[512,18432]{1,0:T(8,128)(2,1)} copy(bf16[512,18432]{1,0:T(8,128)(2,1)} %get-tuple-element.6) | data formatting | bytes 37748736
  (2 shorter events, 0.1 us)
where the time goes:
time: 472 us; the launch traced here: 471 us
  Pallas kernels  446 us (94%)
  local copies, waits for them, and re-layouts  23.6 us (5%)
    pallas_call x1, Pallas kernels, shards(): pl.pallas_call(functools.partial(ladder_kernel, peers, gather), out_shape...  446 us
    unnamed x3, local copies, waits for them, and re-layouts  19.9 us

commit v1 on v0

--- a/solution.py
+++ b/solution.py
@@ -12,31 +12,14 @@
 SLOTS = 3
 
 
-def pair_energy(eps_occ, first_pair, pair_count):
-    occupied = eps_occ.shape[0]
-    pair_index = first_pair + jnp.arange(pair_count, dtype=jnp.int32)
-    first_orbital = pair_index // occupied
-    second_orbital = pair_index % occupied
-    orbitals = jnp.arange(occupied, dtype=jnp.int32)
-    first_energy = jnp.sum(
-        jnp.where(orbitals[None, :] == first_orbital[:, None], eps_occ[None, :], 0.0), axis=1
-    )
-    second_energy = jnp.sum(
-        jnp.where(orbitals[None, :] == second_orbital[:, None], eps_occ[None, :], 0.0), axis=1
-    )
-    return first_energy + second_energy
-
-
 def ladder_kernel(
     peers,
     gather,
     amplitudes,
     integrals,
     rotation,
-    rotation_t,
-    energy,
-    eps_column,
-    eps_row,
+    eps_occ,
+    eps_vir,
     out,
     landed,
     panels,
@@ -47,6 +30,8 @@
     dressed,
     updates,
     packed,
+    rotation_t,
+    eps_first,
     panel_send,
     panel_recv,
     own_sem,
@@ -57,9 +42,10 @@
     update_send,
     update_recv,
 ):
-    chunks, _, width = amplitudes.shape
+    chunks, _, _, width = panels.shape
+    pair_count = amplitudes.shape[1]
     row_count, summed = integrals.shape
-    orbitals = rotation.shape[0]
+    orbitals, occupied = rotation.shape[0], eps_occ.shape[0]
     _, groups, per_owner, group_rows, _ = landed.shape
     chunk_pairs = per_owner // chunks
     first_rows = row_count // orbitals
@@ -93,27 +79,45 @@
         fetch(step).start()
     pl.semaphore_wait(barrier, peers - 1)
 
-    def panel_copy(chunk, step, peer, origin):
+    sibling = me + 1 - 2 * lax.rem(me, 2)
+
+    def own_columns(chunk):
+        return amplitudes.at[:, pl.ds(chunk * width, width)]
+
+    def panel_copy(chunk, index, peer, origin, hand_on):
         return pltpu.make_async_remote_copy(
-            src_ref=amplitudes.at[chunk],
+            src_ref=panels.at[chunk, origin] if hand_on else own_columns(chunk),
             dst_ref=panels.at[chunk, origin],
-            send_sem=panel_send.at[chunk, step],
+            send_sem=panel_send.at[chunk, index],
             recv_sem=panel_recv.at[chunk, origin],
             device_id={"vp": peer},
         )
 
-    def own_panel(chunk):
-        return pltpu.make_async_copy(
-            amplitudes.at[chunk], panels.at[chunk, me if gather else 0], own_sem
-        )
-
-    for chunk in range(chunks):
+    def start_panels(chunk):
         if gather:
-            each_peer(lambda step, peer: panel_copy(chunk, step, peer, me).start())
-        own_panel(chunk).start()
-        own_panel(chunk).wait()
-        if gather and chunk == 0:
-            each_peer(lambda step, peer: panel_copy(0, step, peer, peer).wait_recv())
+            for step in range(2, peers, 2):
+                panel_copy(chunk, step, peer_of(step), me, False).start()
+            panel_copy(chunk, 1, sibling, me, False).start()
+        own = pltpu.make_async_copy(
+            own_columns(chunk), panels.at[chunk, me if gather else 0], own_sem
+        )
+        own.start()
+        own.wait()
+
+    def finish_panels(chunk):
+        for step in range(2, peers, 2):
+            panel_copy(chunk, step, sibling, peer_of(step), True).wait_recv()
+            panel_copy(chunk, step + 1, sibling, peer_of(step), True).start()
+        for step in range(0, peers, 2):
+            panel_copy(chunk, 1, sibling, lax.rem(sibling + step, peers), True).wait_recv()
+
+    start_panels(0)
+    rotation_t[...] = rotation[...].T
+    eps_first[...] = jnp.broadcast_to(eps_vir[...].reshape(1, orbitals), (orbitals, orbitals)).T
+    if gather:
+        finish_panels(0)
+    for chunk in range(1, chunks):
+        start_panels(chunk)
 
     def half_copy(turn, step, peer, origin):
         chunk, group = lax.div(turn, groups), lax.rem(turn, groups)
@@ -134,7 +138,7 @@
 
                 @pl.when(turn == later * groups)
                 def _():
-                    each_peer(lambda step, peer: panel_copy(later, step, peer, peer).wait_recv())
+                    finish_panels(later)
 
         def one_row(row, carry):
             step = turn * group_rows + row
@@ -186,11 +190,15 @@
     turns = chunks * groups
     lax.fori_loop(0, turns, send_turn, 0)
 
+    def first_row(batch, origin):
+        chunk, part = lax.div(batch, per_chunk), lax.rem(batch, per_chunk)
+        return pl.multiple_of(chunk * width + origin * chunk_pairs + part * ROWS, ROWS)
+
     def update_copy(batch, step, peer, origin):
         slot = lax.rem(batch, 2)
         return pltpu.make_async_remote_copy(
             src_ref=updates.at[slot, :, pl.ds(pl.multiple_of(peer * row_count, LANES), row_count)],
-            dst_ref=out.at[pl.ds(pl.multiple_of(origin * per_owner + batch * ROWS, ROWS), ROWS)],
+            dst_ref=out.at[pl.ds(first_row(batch, origin), ROWS)],
             send_sem=update_send.at[slot, step],
             recv_sem=update_recv.at[batch, origin],
             device_id={"vp": peer},
@@ -229,7 +237,9 @@
                         )
                 half = packed[...].astype(jnp.bfloat16)
             full = jnp.dot(rotation_t[...], half, preferred_element_type=jnp.float32)
-            divisor = energy[batch * ROWS + pair] - eps_column[...] - eps_row[...]
+            index = lax.axis_index("ob") * pair_count + first_row(batch, me) + pair
+            energy = eps_occ[lax.div(index, occupied)] + eps_occ[lax.rem(index, occupied)]
+            divisor = energy - eps_first[...] - eps_vir[...].reshape(1, orbitals)
             full = full / divisor
             first = pl.multiple_of(pair * orbitals, orbitals)
             for strip in range(strips):
@@ -256,7 +266,7 @@
         each_peer(lambda step, peer: update_copy(batch, step, peer, me).start())
         own = pltpu.make_async_copy(
             updates.at[slot, :, pl.ds(pl.multiple_of(me * row_count, LANES), row_count)],
-            out.at[pl.ds(pl.multiple_of(me * per_owner + batch * ROWS, ROWS), ROWS)],
+            out.at[pl.ds(first_row(batch, me), ROWS)],
             own_sem,
         )
         own.start()
@@ -267,7 +277,7 @@
 
     if gather:
         for chunk in range(chunks):
-            each_peer(lambda step, peer: panel_copy(chunk, step, peer, me).wait_send())
+            each_peer(lambda step, peer: panel_copy(chunk, step, sibling, me, False).wait_send())
     for turn in range(max(0, turns - 2), turns):
         each_peer(lambda step, peer: half_copy(turn, step, peer, me).wait_send())
     for batch in range(max(0, batches - 2), batches):
@@ -278,6 +288,10 @@
         return carry
 
     lax.fori_loop(0, batches, all_arrived, 0)
+
+
+def copy_kernel(source, target):
+    target[...] = source[...]
 
 
 def shards(integrals, amplitudes, rotation, eps_occ, eps_vir):
@@ -294,17 +308,10 @@
     width = peers * chunk_pairs
     batches = per_owner // ROWS
     turns = chunks * groups
-    gather = depth % ROWS == 0
+    gather = depth % ROWS == 0 and peers % 2 == 0
     if not gather:
         amplitudes = lax.all_gather(amplitudes, "vp", axis=0, tiled=True)
         depth = summed
-    amplitudes = (
-        amplitudes.reshape(depth, peers, chunks, chunk_pairs)
-        .transpose(2, 0, 1, 3)
-        .reshape(chunks, depth, width)
-    )
-    first_pair = lax.axis_index("ob") * pair_count + lax.axis_index("vp") * per_owner
-    energy = pair_energy(eps_occ, first_pair, per_owner)
     bf16, f32 = jnp.bfloat16, jnp.float32
     vmem = pl.BlockSpec(memory_space=pltpu.VMEM)
     anywhere = pl.BlockSpec(memory_space=pl.ANY)
@@ -320,9 +327,7 @@
             anywhere,
             anywhere,
             vmem,
-            vmem,
             pl.BlockSpec(memory_space=pltpu.SMEM),
-            vmem,
             vmem,
         ],
         out_specs=(anywhere, anywhere),
@@ -335,6 +340,8 @@
             pltpu.VMEM((orbitals // LANES, ROWS * orbitals, LANES), f32),
             pltpu.VMEM((2, ROWS, orbitals * orbitals), bf16),
             pltpu.VMEM(spare, f32),
+            pltpu.VMEM((orbitals, orbitals), bf16),
+            pltpu.VMEM((orbitals, orbitals), f32),
             pltpu.SemaphoreType.DMA((chunks, peers)),
             pltpu.SemaphoreType.DMA((chunks, peers)),
             pltpu.SemaphoreType.DMA,
@@ -351,16 +358,19 @@
         compiler_params=pltpu.CompilerParams(
             collective_id=0, has_side_effects=True, vmem_limit_bytes=60 * 1024 * 1024
         ),
-    )(
-        amplitudes,
-        integrals,
-        rotation,
-        rotation.T,
-        energy,
-        eps_vir.reshape(orbitals, 1),
-        eps_vir.reshape(1, orbitals),
-    )
-    return result
+    )(amplitudes, integrals, rotation, eps_occ, eps_vir)
+    block = pl.BlockSpec((2 * ROWS, row_count), lambda step: (step, 0))
+    return pl.pallas_call(
+        copy_kernel,
+        out_shape=jax.ShapeDtypeStruct(result.shape, bf16),
+        grid=(pair_count // (2 * ROWS),),
+        in_specs=[block],
+        out_specs=block,
+        cost_estimate=pl.CostEstimate(
+            flops=0, bytes_accessed=4 * pair_count * row_count, transcendentals=0
+        ),
+        compiler_params=pltpu.CompilerParams(vmem_limit_bytes=60 * 1024 * 1024),
+    )(result)
 
 
 def solution(mesh):

time: 472 us -> 463 us (0.981)
  local copies, waits for them, and re-layouts: 23.6 us -> 0 us
  Pallas kernels: 446 us -> 462 us
    unnamed x3 -> x0, local copies, waits for them, and re-layouts: 19.9 us -> none
    pallas_call x0 -> x1, Pallas kernels: none -> 18.6 us  [shards(): pl.pallas_call(copy_kernel, out_shape=jax.ShapeDtypeStruct(result.shape,...]
where the time goes in v1:
time: 463 us; the launch traced here: 462 us
  Pallas kernels  462 us (100%)
    pallas_call x1, Pallas kernels, shards(): pl.pallas_call(functools.partial(ladder_kernel, peers, gather), out_shape...  443 us
    pallas_call x1, Pallas kernels, shards(): pl.pallas_call(copy_kernel, out_shape=jax.ShapeDtypeStruct(result.shape,...  18.6 us

profile of v1, /device:TPU:1, one launch (start us, length us, event | category | flops | bytes accessed | tf_op | source)
XLA Modules:
  0.0 461.8 jit_solution(15430976822104388938)
XLA Ops:
  0.0 443.2 %shard_map.55 = (bf16[512,18432]{1,0:T(8,128)(2,1)}, bf16[8,3,64,16,384]{4,3,2,1,0:T(8,128)(2,1)}) custom-call(bf16[288,512]{1,0:T(8,128)(2,1)} %amplitudes.1, bf16[18432,2304]{1,0:T(8,128)(2,1)} %integrals.1, bf16[384,384]{1,0:T(8,128)(2,1)} %rotation.1, f32[64]{0:T(128)} %eps_occ.1, f32[384]{0:T(512)} %eps_vir.1), custom_call_target="tpu_custom_call" | custom-call | flops 57982058496 | bytes 169869312 | tf_op jit(solution)/shard_map/pallas_call | solution.py:320
  443.2 18.6 %shard_map.56 = bf16[512,18432]{1,0:T(8,128)(2,1)} custom-call(bf16[512,18432]{1,0:T(8,128)(2,1)} %get-tuple-element.6.source), custom_call_target="tpu_custom_call" | custom-call | bytes 37748736 | tf_op jit(solution)/shard_map/pallas_call | solution.py:363

commit v2 on v1

--- a/solution.py
+++ b/solution.py
@@ -9,7 +9,7 @@
 
 LANES = 128
 ROWS = 16
-SLOTS = 3
+SLOTS = 6
 
 
 def ladder_kernel(
@@ -27,7 +27,6 @@
     spread,
     sending,
     halves,
-    dressed,
     updates,
     packed,
     rotation_t,
@@ -243,7 +242,7 @@
             full = full / divisor
             first = pl.multiple_of(pair * orbitals, orbitals)
             for strip in range(strips):
-                dressed[strip, pl.ds(first, orbitals), :] = full[
+                spread[strip, pl.ds(first, orbitals), :] = full[
                     :, strip * LANES : (strip + 1) * LANES
                 ]
             return carry
@@ -257,7 +256,7 @@
         def lay_out(orbital, carry):
             for strip in range(strips):
                 column = pl.multiple_of(orbital * orbitals + strip * LANES, LANES)
-                updates[slot, :, pl.ds(column, LANES)] = dressed[
+                updates[slot, :, pl.ds(column, LANES)] = spread[
                     strip, pl.ds(orbital, ROWS, stride=orbitals), :
                 ].astype(jnp.bfloat16)
             return carry
@@ -290,8 +289,26 @@
     lax.fori_loop(0, batches, all_arrived, 0)
 
 
-def copy_kernel(source, target):
-    target[...] = source[...]
+def copy_kernel(source, target, parts, in_sem, out_sem):
+    count, rows, _ = parts.shape
+
+    def read(part):
+        return pltpu.make_async_copy(
+            source.at[pl.ds(part * rows, rows)], parts.at[part], in_sem.at[part]
+        )
+
+    def write(part):
+        return pltpu.make_async_copy(
+            parts.at[part], target.at[pl.ds(part * rows, rows)], out_sem.at[part]
+        )
+
+    for part in range(count):
+        read(part).start()
+    for part in range(count):
+        read(part).wait()
+        write(part).start()
+    for part in range(count):
+        write(part).wait()
 
 
 def shards(integrals, amplitudes, rotation, eps_occ, eps_vir):
@@ -334,10 +351,11 @@
         scratch_shapes=[
             pltpu.VMEM((chunks, summed // depth, depth, width), bf16),
             pltpu.VMEM((SLOTS, orbitals, summed), bf16),
-            pltpu.VMEM((orbitals // LANES, width * group_rows, LANES), f32),
+            pltpu.VMEM(
+                (orbitals // LANES, max(width * group_rows, ROWS * orbitals), LANES), f32
+            ),
             pltpu.VMEM((2, width, group_rows, orbitals), bf16),
             pltpu.VMEM((peers, groups, ROWS, group_rows, orbitals), bf16),
-            pltpu.VMEM((orbitals // LANES, ROWS * orbitals, LANES), f32),
             pltpu.VMEM((2, ROWS, orbitals * orbitals), bf16),
             pltpu.VMEM(spare, f32),
             pltpu.VMEM((orbitals, orbitals), bf16),
@@ -359,13 +377,17 @@
             collective_id=0, has_side_effects=True, vmem_limit_bytes=60 * 1024 * 1024
         ),
     )(amplitudes, integrals, rotation, eps_occ, eps_vir)
-    block = pl.BlockSpec((2 * ROWS, row_count), lambda step: (step, 0))
+    parts = pair_count // (2 * ROWS)
     return pl.pallas_call(
         copy_kernel,
         out_shape=jax.ShapeDtypeStruct(result.shape, bf16),
-        grid=(pair_count // (2 * ROWS),),
-        in_specs=[block],
-        out_specs=block,
+        in_specs=[anywhere],
+        out_specs=anywhere,
+        scratch_shapes=[
+            pltpu.VMEM((parts, 2 * ROWS, row_count), bf16),
+            pltpu.SemaphoreType.DMA((parts,)),
+            pltpu.SemaphoreType.DMA((parts,)),
+        ],
         cost_estimate=pl.CostEstimate(
             flops=0, bytes_accessed=4 * pair_count * row_count, transcendentals=0
         ),

time: 463 us -> 457 us (0.987)
  Pallas kernels: 462 us -> 456 us
    pallas_call x1, Pallas kernels: 18.6 us -> 13.3 us  [shards(): pl.pallas_call(copy_kernel, out_shape=jax.ShapeDtypeStruct(result.shape,...]
where the time goes in v2:
time: 457 us; the launch traced here: 456 us
  Pallas kernels  456 us (100%)
    pallas_call x1, Pallas kernels, shards(): pl.pallas_call(functools.partial(ladder_kernel, peers, gather), out_shape...  443 us
    pallas_call x1, Pallas kernels, shards(): pl.pallas_call(copy_kernel, out_shape=jax.ShapeDtypeStruct(result.shape,...  13.3 us

profile of v2, /device:TPU:1, one launch (start us, length us, event | category | flops | bytes accessed | tf_op | source)
XLA Modules:
  0.0 456.5 jit_solution(14013553850213676831)
XLA Ops:
  0.0 443.2 %shard_map.55 = (bf16[512,18432]{1,0:T(8,128)(2,1)}, bf16[8,3,64,16,384]{4,3,2,1,0:T(8,128)(2,1)}) custom-call(bf16[288,512]{1,0:T(8,128)(2,1)} %amplitudes.1, bf16[18432,2304]{1,0:T(8,128)(2,1)} %integrals.1, bf16[384,384]{1,0:T(8,128)(2,1)} %rotation.1, f32[64]{0:T(128)} %eps_occ.1, f32[384]{0:T(512)} %eps_vir.1), custom_call_target="tpu_custom_call" | custom-call | flops 57982058496 | bytes 169869312 | tf_op jit(solution)/shard_map/pallas_call | solution.py:337
  443.2 13.3 %shard_map.56 = bf16[512,18432]{1,0:T(8,128)(2,1)} custom-call(bf16[512,18432]{1,0:T(8,128)(2,1)} %get-tuple-element.6.source), custom_call_target="tpu_custom_call" | custom-call | bytes 37748736 | tf_op jit(solution)/shard_map/pallas_call | solution.py:381
